TPU v7x, 256 devices: a whole 4x4x8 slice. The times are simulated.
256 devices in a mesh: member: 16 (over y, z_lo), grid: 16 (over z_hi, x, core).
Axes of the slice: x: 4, y: 4, z: 8 (z_hi: 2, z_lo: 4; z = z_hi * 4 + z_lo), core: 2. Of those that a mesh axis runs over, the one named last changes fastest.
Arguments:
- latents: bfloat16 [16, 16384, 1024], P('member', 'grid'), may hold values from -6 to 6
- w_in: bfloat16 [1024, 1024], replicated, may hold values from -0.1875 to 0.1875
- b_in: float32 [1024], replicated, may hold values from -3 to 3
- w_out: bfloat16 [1024, 96], replicated, may hold values from -0.1875 to 0.1875
- b_out: float32 [96], replicated, may hold values from -3 to 3
- target: float32 [96, 16384], P('member', 'grid'), may hold values from -6 to 6
- area_weight: float32 [16384], P('grid'), may hold values from 0.25 to 10
- var_weight: float32 [96], P('member'), may hold values from 0.25 to 10
- smoothers: float32 [2, 128, 4, 128, 128], P(None, 'grid'), may hold values from -0.25 to 0.25
- block_index: int32 [2, 128, 4], P(None, 'grid'), may hold values from 0 to 127, as said below
- block_count: int32 [2, 128], P(None, 'grid'), may hold values from 1 to 4, as said below
Outputs:
- grad_latent: bfloat16 [16, 16384, 1024], P('member', 'grid')
- loss: float32 [], replicated
Inputs may be any that keep to these rules, and one draw needn't show every extreme that they name: `block_index`: block row r lists blocks that lie at most 8 blocks from r on either side; that distance is reached on both sides in some rows; entries of a row may repeat. Only the first block_count[s, r] slots of block row r are used.
All inputs are finite; a program needn't handle non-finite values.
Results may differ from a plain program's by a relative error of at most 0.008.
Values may be sent and summed in bfloat16 or wider, within the bound.
A program may use at most 64 MiB of HBM per device.

v0:
```python
import math

import jax
import jax.numpy as jnp
from jax import lax
from jax.sharding import PartitionSpec as P

kernel_eps = 0.01
highest = lax.Precision.HIGHEST


def passed_along(block, axis, distance):
    devices = range(lax.axis_size(axis))
    route = [(i - distance, i) for i in devices if i - distance in devices]
    return lax.ppermute(block, axis, route)


def extended_2(cells, sides, width):
    for axis, dim in sides:
        count = lax.axis_size(axis)
        ends = count - 1
        head = lax.slice_in_dim(cells, 0, width, axis=dim)
        tail = lax.slice_in_dim(cells, cells.shape[dim] - width, cells.shape[dim], axis=dim)
        cells = jnp.concatenate(
            [
                lax.ppermute(tail, axis, [(i, (i + 1) % count) for i in range(ends)]),
                cells,
                lax.ppermute(head, axis, [((i + 1) % count, i) for i in range(ends)]),
            ],
            axis=dim,
        )
    return cells


def block_weights(smoothers, counts):
    slots = smoothers.shape[2]
    live = (jnp.arange(slots, dtype=jnp.int32)[None, None, :] < counts[:, :, None]).astype(
        jnp.float32
    )
    return smoothers * live[:, :, :, None, None]


def smooth_local(extended, masked, positions):
    height = extended.shape[0]
    blocks_dev = masked.shape[0]
    block_size = masked.shape[2]
    blocks = extended.reshape(height, 3 * blocks_dev, block_size)
    picked = jnp.take(blocks, positions, axis=1).astype(jnp.float32)
    result = jnp.einsum("rbkp,bkpq->rbq", picked, masked, precision=highest)
    return result.reshape(height, blocks_dev * block_size)


def adjoint_local(grad_rows, masked, positions):
    height = grad_rows.shape[0]
    blocks_dev = masked.shape[0]
    block_size = masked.shape[2]
    blocks = grad_rows.reshape(height, blocks_dev, block_size)
    contrib = jnp.einsum("rbq,bkpq->rbkp", blocks, masked, precision=highest)
    onehot = (
        positions[:, :, None] == jnp.arange(3 * blocks_dev, dtype=jnp.int32)[None, None, :]
    ).astype(jnp.float32)
    result = jnp.einsum("rbkp,bkc->rcp", contrib, onehot, precision=highest)
    return result.reshape(height, 3 * blocks_dev * block_size)


def fold_rims(extended, width):
    center = extended[:, width : 2 * width]
    from_upper = passed_along(extended[:, :width], "grid", -1)
    from_lower = passed_along(extended[:, 2 * width :], "grid", 1)
    return center + from_upper + from_lower


def ensemble_loss(fields, truth, weight_grid):
    members = fields.shape[0]
    spread = fields[:, None] - fields[None, :]
    kernel = jnp.sqrt(spread * spread + kernel_eps)
    miss = fields - truth[None]
    kernel_miss = jnp.sqrt(miss * miss + kernel_eps)
    score = jnp.mean(kernel_miss, 0) - (
        jnp.sum(kernel, (0, 1)) - members * math.sqrt(kernel_eps)
    ) / (2.0 * members * (members - 1))
    total = jnp.sum(weight_grid * score)
    grad = weight_grid[None] * (miss / kernel_miss - jnp.sum(spread / kernel, 1) / (members - 1))
    return (total, grad)


def ensemble_terms(layers, truths, weight_grid):
    total = jnp.zeros((), jnp.float32)
    grads = []
    for layer_field, layer_truth in zip(layers, truths):
        part_total, grad = ensemble_loss(layer_field, layer_truth, weight_grid)
        total = total + part_total
        grads.append(grad)
    return (total, grads)


def on_device(
    latents,
    w_in,
    b_in,
    w_out,
    b_out,
    target,
    area_weight,
    var_weight,
    smoothers,
    block_index,
    block_count,
):
    member_count, points, latent_width = latents.shape
    var_total = w_out.shape[1]
    scale_count = smoothers.shape[0]
    blocks_dev = smoothers.shape[1]
    latent_rows = latents.reshape(member_count * points, latent_width)
    pre_act = jnp.dot(latent_rows, w_in, preferred_element_type=jnp.float32) + b_in
    hidden = jax.nn.gelu(pre_act).astype(jnp.bfloat16)
    hidden_width = hidden.shape[1]
    predicted = (
        jnp.einsum(
            "mph,hv->mvp",
            hidden.reshape(member_count, points, hidden_width),
            w_out,
            preferred_element_type=jnp.float32,
        )
        + b_out[None, :, None]
    )
    masked = block_weights(smoothers, block_count)
    positions = block_index - (lax.axis_index("grid") - 1) * blocks_dev
    weight_grid = var_weight[:, None] * area_weight[None, :]
    field_count = member_count * var_total
    joint = jnp.concatenate(
        [predicted.reshape(field_count, points).astype(jnp.bfloat16), target.astype(jnp.bfloat16)],
        0,
    )
    extended = extended_2(joint, (("grid", 1),), points)
    layers = [predicted]
    truths = [target]
    for scale in range(scale_count):
        smoothed = smooth_local(extended, masked[scale], positions[scale])
        layers.append(smoothed[:field_count].reshape(member_count, var_total, points))
        truths.append(smoothed[field_count:])
    joined = lax.all_to_all(jnp.stack(layers), "member", split_axis=2, concat_axis=1, tiled=True)
    total, grads = ensemble_terms(
        [joined[layer] for layer in range(scale_count + 1)], truths, weight_grid
    )
    returned = lax.all_to_all(jnp.stack(grads), "member", split_axis=1, concat_axis=2, tiled=True)
    adjoint = adjoint_local(returned[1].reshape(field_count, points), masked[0], positions[0])
    scale = 1
    adjoint = adjoint + adjoint_local(
        returned[scale + 1].reshape(field_count, points), masked[scale], positions[scale]
    )
    field_grad = returned[0] + fold_rims(adjoint, points).reshape(member_count, var_total, points)
    loss_sum = lax.psum(total, ("member", "grid"))
    loss = loss_sum / ((scale_count + 1) * var_total * points * lax.axis_size("grid"))
    grad_low = field_grad.astype(jnp.bfloat16)
    hidden_grad = jnp.einsum(
        "mvp,hv->mph", grad_low, w_out, preferred_element_type=jnp.float32
    ).reshape(member_count * points, hidden_width)
    _, gelu_back = jax.vjp(jax.nn.gelu, pre_act)
    pre_grad = gelu_back(hidden_grad)[0].astype(jnp.bfloat16)
    latent_grad = lax.dot_general(
        pre_grad, w_in, (((1,), (1,)), ((), ())), preferred_element_type=jnp.float32
    )
    return (latent_grad.astype(jnp.bfloat16).reshape(member_count, points, latent_width), loss)


def solution(mesh):
    in_specs = (
        P("member", "grid", None),
        P(),
        P(),
        P(),
        P(),
        P("member", "grid"),
        P("grid"),
        P("member"),
        P(None, "grid", None, None, None),
        P(None, "grid", None),
        P(None, "grid"),
    )
    out_specs = (P("member", "grid", None), P())
    return jax.shard_map(
        on_device, mesh=mesh, in_specs=in_specs, out_specs=out_specs, check_vma=False
    )
```

profile of v0, /device:TPU:1, one launch (start us, length us, event | category | flops | bytes accessed | tf_op | source)
XLA Modules:
  0.0 264.8 jit_solution(11075591352670561546)
XLA Ops:
  2.2 4.0 %fusion.20 = f32[1024,1024]{1,0:T(8,128)S(1)} fusion(bf16[1024,1024]{1,0:T(8,128)(2,1)S(1)} %copy-done, bf16[1,1024,1024]{2,1,0:T(8,128)(2,1)} %param.13), kind=kOutput, calls=%fused_computation.33 | convolution fusion | flops 2147483648 | bytes 8388608 | tf_op jit(solution)/shard_map/dot_general | solution.py:115
  6.3 2.5 bitcast_convert_fusion
  8.7 5.2 %collective-permute-start.1 = (bf16[102,1024]{1,0:T(8,128)(2,1)S(1)}, bf16[102,1024]{1,0:T(8,128)(2,1)S(1)}, u32[]{:S(2)}, u32[]{:S(2)}) collective-permute-start(bf16[102,1024]{1,0:T(8,128)(2,1)S(1)} %pad_maximum_fusion.3), channel_id=1, source_target_pairs={{1,0},{2,1},{3,2},{4,3},{5,4},{6,5},{7,6},{8,7},{9,8},{10,9},{11,1... | collective-permute-start | bytes 626696 | tf_op jit(solution)/shard_map/ppermute | solution.py:28
  13.9 1.9 collective-permute-start
  16.5 4.5 %broadcast_multiply_fusion = f32[2,8,4,128,128]{4,3,2,1,0:T(8,128)} fusion(f32[2,8,4,128,128]{4,3,2,1,0:T(8,128)} %param.21, f32[2,8,4]{2,1,0:T(8,128)S(1)} %fusion.79), kind=kLoop, calls=%fused_computation.38 | loop fusion | flops 1048576 | bytes 8388864 | tf_op jit(solution)/shard_map/mul | solution.py:40
  22.9 3.0 %fusion.49 = f32[102,8,128]{2,0,1:T(8,128)S(1)} fusion(f32[2,8,4,128,128]{4,3,2,1,0:T(8,128)} %broadcast_multiply_fusion, bf16[8,4,102,128]{3,2,1,0:T(8,128)(2,1)} %bitcast.116, pred[8,4]{1,0:T(8,128)(4,1)S(1)} %copy.152), kind=kOutput, calls=%fused_computation.58 | convolution fusion | flops 642146304 | bytes 3366944 | tf_op jit(solution)/shard_map/rbkp,bkpq->rbq/dot_general | solution.py:49
  28.6 3.0 %fusion.50 = f32[102,8,128]{2,0,1:T(8,128)S(1)} fusion(f32[2,8,4,128,128]{4,3,2,1,0:T(8,128)} %broadcast_multiply_fusion, bf16[8,4,102,128]{3,2,1,0:T(8,128)(2,1)} %bitcast.115, pred[8,4]{1,0:T(8,128)(4,1)S(1)} %copy.148), kind=kOutput, calls=%fused_computation.59 | convolution fusion | flops 642146304 | bytes 3366944 | tf_op jit(solution)/shard_map/rbkp,bkpq->rbq/dot_general | solution.py:49
  33.8 2.2 copy.156
  36.0 7.7 %all-to-all-start = ((f32[3,1,96,1024]{3,1,0,2:T(1,128)}), f32[3,1,96,1024]{3,1,0,2:T(1,128)S(1)}, u32[]{:S(2)}, u32[]{:S(2)}) async-start(f32[3,1,96,1024]{3,1,0,2:T(1,128)} %copy.156), calls=%async_computation | async-start | bytes 2359296 | tf_op jit(solution)/shard_map/all_to_all | solution.py:142
  46.5 28.9 %all-to-all-done = f32[3,1,96,1024]{3,1,0,2:T(1,128)S(1)} async-done(((f32[3,1,96,1024]{3,1,0,2:T(1,128)}), f32[3,1,96,1024]{3,1,0,2:T(1,128)S(1)}, u32[]{:S(2)}, u32[]{:S(2)}) %all-to-all-start) | async-done | bytes 1179680 | tf_op jit(solution)/shard_map/all_to_all | solution.py:142
  75.4 4.6 %slice_reduce_fusion.2 = (f32[96,1024]{1,0:T(8,128)}, f32[96,1024]{1,0:T(8,128)}, f32[96,1024]{1,0:T(8,128)}, f32[1,1,96,1024]{3,1,0,2:T(1,128)}, f32[1,1,96,1024]{3,1,0,2:T(1,128)}, /*index=5*/f32[1,1,96,1024]{3,1,0,2:T(1,128)}) fusion(f32[3,1,96,1024]{3,1,0,2:T(1,128)S(1)} %all-to-all-done), kind=kLoop, calls=%fused_computation.136 | loop fusion | bytes 3538944 | tf_op jit(solution)/shard_map/slice | solution.py:144
  87.9 5.6 %fusion.10 = (f32[6,1024]{1,0:T(8,128)S(1)}, f32[16,6,1024]{2,1,0:T(8,128)S(1)}) fusion(f32[16,6,1024]{2,0,1:T(8,128)S(1)} %copy.164, f32[16,6,1024]{2,1,0:T(8,128)} %sub.198), kind=kLoop, calls=%fused_computation.18 | loop fusion | flops 9332736 | bytes 1204224 | tf_op jit(solution)/shard_map/reduce_sum | solution.py:80
  93.6 11.1 %fusion.2 = (f32[6,1024]{1,0:T(8,128)S(1)}, f32[16,6,1024]{2,1,0:T(8,128)S(1)}, f32[16,6,1024]{2,1,0:T(8,128)S(1)}, f32[6,1024]{1,0:T(8,128)S(1)}) fusion(f32[16,6,1024]{2,0,1:T(8,128)} %copy.158, f32[16,6,1024]{2,1,0:T(8,128)S(1)} %sub.182, f32[16,6,1024]{2,0,1:T(8,128)} %copy.161, f32[16,6,1024]{2,1,0:T(8,128)S(1)} %sub.190), kind=kLoop, calls=%fused_computation.10 | loop fusion | flops 18665472 | bytes 2408448 | tf_op jit(solution)/shard_map/reduce_sum | solution.py:80
  107.3 1.9 copy.166
  109.1 4.4 %all-to-all-start.1 = ((f32[3,16,6,1024]{3,2,0,1:T(8,128)}), f32[3,16,6,1024]{3,2,0,1:T(8,128)}, u32[]{:S(2)}, u32[]{:S(2)}) async-start(f32[3,16,6,1024]{3,2,0,1:T(8,128)} %copy.166), calls=%async_computation.1 | async-start | bytes 3145728 | tf_op jit(solution)/shard_map/all_to_all | solution.py:146
  113.6 38.6 %all-to-all-done.1 = f32[3,16,6,1024]{3,2,0,1:T(8,128)} async-done(((f32[3,16,6,1024]{3,2,0,1:T(8,128)}), f32[3,16,6,1024]{3,2,0,1:T(8,128)}, u32[]{:S(2)}, u32[]{:S(2)}) %all-to-all-start.1) | async-done | bytes 1179680 | tf_op jit(solution)/shard_map/all_to_all | solution.py:146
  152.1 2.3 fusion.92
  154.6 3.8 %fusion.39 = f32[96,8,4,128]{3,0,2,1:T(8,128)S(1)} fusion(f32[2,8,4,128,128]{4,3,2,1,0:T(8,128)} %broadcast_multiply_fusion, f32[96,8,128,1]{2,1,0,3:T(8,128)S(1)} %bitcast.125), kind=kOutput, calls=%fused_computation.54 | convolution fusion | flops 603979776 | bytes 4063232 | tf_op jit(solution)/shard_map/rbq,bkpq->rbkp/dot_general | solution.py:58
  158.4 3.8 %fusion.38 = f32[96,8,4,128]{3,0,2,1:T(8,128)S(1)} fusion(f32[2,8,4,128,128]{4,3,2,1,0:T(8,128)} %broadcast_multiply_fusion, f32[96,8,128,1]{2,1,0,3:T(8,128)S(1)} %bitcast.124), kind=kOutput, calls=%fused_computation.53 | convolution fusion | flops 603979776 | bytes 4063232 | tf_op jit(solution)/shard_map/rbq,bkpq->rbkp/dot_general | solution.py:58
  166.8 3.3 %collective-permute-start.2 = (f32[96,1024]{1,0:T(8,128)}, f32[96,1024]{1,0:T(8,128)}, u32[]{:S(2)}, u32[]{:S(2)}) collective-permute-start(f32[96,1024]{1,0:T(8,128)} %get-tuple-element.18), channel_id=1, source_target_pairs={{1,0},{2,1},{3,2},{4,3},{5,4},{6,5},{7,6},{8,7},{9,8},{10,9},{11,1... | collective-permute-start | bytes 1179656 | tf_op jit(solution)/shard_map/ppermute | solution.py:15
  170.2 3.1 %collective-permute-start.3 = (f32[96,1024]{1,0:T(8,128)}, f32[96,1024]{1,0:T(8,128)}, u32[]{:S(2)}, u32[]{:S(2)}) collective-permute-start(f32[96,1024]{1,0:T(8,128)} %get-tuple-element.19), channel_id=1, source_target_pairs={{0,1},{1,2},{2,3},{3,4},{4,5},{5,6},{6,7},{7,8},{8,9},{9,10},{10,1... | collective-permute-start | bytes 1179656 | tf_op jit(solution)/shard_map/ppermute | solution.py:15
  175.0 78.4 %psum.7 = f32[]{:T(128)} all-reduce(f32[]{:T(128)S(6)} %add.145), channel_id=1, replica_groups=mesh['member'=16,'grid'=16] {'member','grid'}, use_global_device_ids=true, to_apply=%region_12.14 | all-reduce | flops 1 | bytes 8 | tf_op jit(solution)/shard_map/psum | solution.py:153
  254.0 1.8 squeeze.33
  255.8 7.9 %convert_bitcast_fusion = bf16[1,1024,1024]{2,1,0:T(8,128)(2,1)} fusion(bf16[1024,1024]{1,0:T(8,128)(2,1)S(1)} %copy-done, f32[1024,1024]{1,0:T(8,128)} %copy-done.20, bf16[1024,96]{0,1:T(8,128)(2,1)S(1)} %copy-done.17, f32[1024]{0:T(1024)S(1)} %copy-done.18, f32[96,1024]{1,0:T(8,128)} %squeeze.33, f32[96,1024]{1,0:T(8,128)} %collective-permute-done.3, ...), kind=kOutput, calls=%fused_computation.35 | convolution fusion | flops 2372272128 | bytes 10162176 | tf_op jit(solution)/shard_map/dot_general | solution.py:161
  (93 shorter events, 26.8 us)
Async XLA Ops:
  2.2 4.0 %copy-start.16 = (bf16[1024,96]{0,1:T(8,128)(2,1)S(1)}, bf16[1024,96]{0,1:T(8,128)(2,1)}, u32[]{:S(2)}) copy-start(bf16[1024,96]{0,1:T(8,128)(2,1)} %param.16) | copy-start | bytes 589828
  2.2 4.0 %copy-start.18 = (f32[1024]{0:T(1024)S(1)}, f32[1024]{0:T(1024)}, u32[]{:S(2)}) copy-start(f32[1024]{0:T(1024)} %param.15) | copy-start | bytes 12292
  2.2 4.0 %copy-start.19 = (f32[96]{0:T(128)S(1)}, f32[96]{0:T(128)}, u32[]{:S(2)}) copy-start(f32[96]{0:T(128)} %param.17) | copy-start | bytes 1156
  6.2 2.5 copy-start.20
  6.2 9.6 %copy-start.13 = (s32[2,8,4]{1,2,0:T(4,128)S(1)}, s32[2,8,4]{1,2,0:T(4,128)}, u32[]{:S(2)}) copy-start(s32[2,8,4]{1,2,0:T(4,128)} %param.22) | copy-start | bytes 772
  6.3 10.1 %copy-start.14 = (s32[2,8]{1,0:T(2,128)S(1)}, s32[2,8]{1,0:T(2,128)}, u32[]{:S(2)}) copy-start(s32[2,8]{1,0:T(2,128)} %param.23) | copy-start | bytes 196
  8.7 12.3 %collective-permute-start.1 = (bf16[102,1024]{1,0:T(8,128)(2,1)S(1)}, bf16[102,1024]{1,0:T(8,128)(2,1)S(1)}, u32[]{:S(2)}, u32[]{:S(2)}) collective-permute-start(bf16[102,1024]{1,0:T(8,128)(2,1)S(1)} %pad_maximum_fusion.3), channel_id=1, source_target_pairs={{1,0},{2,1},{3,2},{4,3},{5,4},{6,5},{7,6},{8,7},{9,8},{10,9},{11,1... | collective-permute-start | bytes 626696 | tf_op jit(solution)/shard_map/ppermute | solution.py:28
  13.9 7.1 %collective-permute-start = (bf16[102,1024]{1,0:T(8,128)(2,1)S(1)}, bf16[102,1024]{1,0:T(8,128)(2,1)S(1)}, u32[]{:S(2)}, u32[]{:S(2)}) collective-permute-start(bf16[102,1024]{1,0:T(8,128)(2,1)S(1)} %pad_maximum_fusion.3), channel_id=1, source_target_pairs={{0,1},{1,2},{2,3},{3,4},{4,5},{5,6},{6,7},{7,8},{8,9},{9,10},{10,1... | collective-permute-start | bytes 626696 | tf_op jit(solution)/shard_map/ppermute | solution.py:26
  36.0 39.4 %all-to-all-start = ((f32[3,1,96,1024]{3,1,0,2:T(1,128)}), f32[3,1,96,1024]{3,1,0,2:T(1,128)S(1)}, u32[]{:S(2)}, u32[]{:S(2)}) async-start(f32[3,1,96,1024]{3,1,0,2:T(1,128)} %copy.156), calls=%async_computation | async-start | bytes 2359296 | tf_op jit(solution)/shard_map/all_to_all | solution.py:142
  80.1 5.7 %copy-start.4 = (f32[96,1024]{1,0:T(8,128)S(1)}, f32[96,1024]{1,0:T(8,128)}, u32[]{:S(2)}) copy-start(f32[96,1024]{1,0:T(8,128)} %get-tuple-element.5) | copy-start | bytes 1179652
  87.9 16.9 %copy-start.1 = (f32[16,6,1024]{2,1,0:T(8,128)S(1)}, f32[16,6,1024]{2,1,0:T(8,128)}, u32[]{:S(2)}) copy-start(f32[16,6,1024]{2,1,0:T(8,128)} %sub.198) | copy-start | bytes 1179652
  87.9 16.8 %copy-start.9 = (f32[6,1024]{1,0:T(8,128)S(1)}, f32[6,1024]{1,0:T(8,128)}, u32[]{:S(2)}) copy-start(f32[6,1024]{1,0:T(8,128)} %slice_bitcast_fusion.14) | copy-start | bytes 73732
  87.9 16.8 %copy-start.10 = (f32[6,1024]{1,0:T(8,128)S(1)}, f32[6,1024]{1,0:T(8,128)}, u32[]{:S(2)}) copy-start(f32[6,1024]{1,0:T(8,128)} %slice_bitcast_fusion.15) | copy-start | bytes 73732
  93.6 11.6 %copy-start.11 = (f32[6,1024]{1,0:T(8,128)S(1)}, f32[6,1024]{1,0:T(8,128)}, u32[]{:S(2)}) copy-start(f32[6,1024]{1,0:T(8,128)} %sqrt_reduce_fusion.2) | copy-start | bytes 73732
  93.6 11.6 %copy-start.12 = (f32[1024]{0:T(1024)S(1)}, f32[1024]{0:T(1024)}, u32[]{:S(2)}) copy-start(f32[1024]{0:T(1024)} %param.19) | copy-start | bytes 12292
  93.6 11.6 %copy-start.15 = (f32[6]{0:T(128)S(1)}, f32[6]{0:T(128)}, u32[]{:S(2)}) copy-start(f32[6]{0:T(128)} %param.20) | copy-start | bytes 76
  93.6 12.3 %copy-start.5 = (f32[1,1,96,1024]{3,1,0,2:T(1,128)S(1)}, f32[1,1,96,1024]{3,1,0,2:T(1,128)}, u32[]{:S(2)}) copy-start(f32[1,1,96,1024]{3,1,0,2:T(1,128)} %get-tuple-element.20) | copy-start | bytes 1179652
  93.6 12.3 %copy-start.6 = (f32[1,1,96,1024]{3,1,0,2:T(1,128)S(1)}, f32[1,1,96,1024]{3,1,0,2:T(1,128)}, u32[]{:S(2)}) copy-start(f32[1,1,96,1024]{3,1,0,2:T(1,128)} %get-tuple-element.21) | copy-start | bytes 1179652
  93.6 12.3 %copy-start.7 = (f32[1,1,96,1024]{3,1,0,2:T(1,128)S(1)}, f32[1,1,96,1024]{3,1,0,2:T(1,128)}, u32[]{:S(2)}) copy-start(f32[1,1,96,1024]{3,1,0,2:T(1,128)} %get-tuple-element.22) | copy-start | bytes 1179652
  93.6 12.3 %copy-start.8 = (f32[6,1024]{1,0:T(8,128)S(1)}, f32[6,1024]{1,0:T(8,128)}, u32[]{:S(2)}) copy-start(f32[6,1024]{1,0:T(8,128)} %param.18) | copy-start | bytes 73732
  109.1 43.0 %all-to-all-start.1 = ((f32[3,16,6,1024]{3,2,0,1:T(8,128)}), f32[3,16,6,1024]{3,2,0,1:T(8,128)}, u32[]{:S(2)}, u32[]{:S(2)}) async-start(f32[3,16,6,1024]{3,2,0,1:T(8,128)} %copy.166), calls=%async_computation.1 | async-start | bytes 3145728 | tf_op jit(solution)/shard_map/all_to_all | solution.py:146
  164.0 91.9 %copy-start.17 = (bf16[1024,96]{0,1:T(8,128)(2,1)S(1)}, bf16[1024,96]{0,1:T(8,128)(2,1)}, u32[]{:S(2)}) copy-start(bf16[1024,96]{0,1:T(8,128)(2,1)} %param.16) | copy-start | bytes 589828
  166.8 89.0 %collective-permute-start.2 = (f32[96,1024]{1,0:T(8,128)}, f32[96,1024]{1,0:T(8,128)}, u32[]{:S(2)}, u32[]{:S(2)}) collective-permute-start(f32[96,1024]{1,0:T(8,128)} %get-tuple-element.18), channel_id=1, source_target_pairs={{1,0},{2,1},{3,2},{4,3},{5,4},{6,5},{7,6},{8,7},{9,8},{10,9},{11,1... | collective-permute-start | bytes 1179656 | tf_op jit(solution)/shard_map/ppermute | solution.py:15
  170.2 85.7 %collective-permute-start.3 = (f32[96,1024]{1,0:T(8,128)}, f32[96,1024]{1,0:T(8,128)}, u32[]{:S(2)}, u32[]{:S(2)}) collective-permute-start(f32[96,1024]{1,0:T(8,128)} %get-tuple-element.19), channel_id=1, source_target_pairs={{0,1},{1,2},{2,3},{3,4},{4,5},{5,6},{6,7},{7,8},{8,9},{9,10},{10,1... | collective-permute-start | bytes 1179656 | tf_op jit(solution)/shard_map/ppermute | solution.py:15
  (3 other events, 3.2 us)
where the time goes:
time: 266 us; the launch traced here: 265 us
  blocking collectives  78.4 us (29%)
  waiting for transfers between devices  67.5 us (25%)
  matrix products  31.2 us (12%)
  local copies, waits for them, and re-layouts  30.1 us (11%)
  other arithmetic  27.4 us (10%)
  starting transfers between devices  25.6 us (10%)
  between operations  4.69 us (2%)
    psum x1, blocking collectives, on_device(): loss_sum = lax.psum(total, ('member', 'grid'))  78.4 us
    all_to_all x1, waiting for transfers between devices, on_device(): lax.all_to_all(jnp.stack(grads), 'member', split_axis=1, concat_axis=2, t...  38.6 us
    all_to_all x1, waiting for transfers between devices, on_device(): lax.all_to_all(jnp.stack(layers), 'member', split_axis=2, concat_axis=1,...  28.9 us
    reduce_sum x2, other arithmetic, ensemble_loss(): jnp.sum(kernel, (0, 1)) - members * math.sqrt(kernel_eps)  16.7 us
    dot_general x1, matrix products, on_device(): lax.dot_general(pre_grad, w_in, (((1,), (1,)), ((), ())), preferred_eleme...  7.86 us
    all_to_all x1, starting transfers between devices, on_device(): lax.all_to_all(jnp.stack(layers), 'member', split_axis=2, concat_axis=1,...  7.72 us
    dot_general x2, matrix products, adjoint_local(): contrib = jnp.einsum('rbq,bkpq->rbkp', blocks, masked, precision=highest)  7.66 us
    ppermute x2, starting transfers between devices, passed_along(): return lax.ppermute(block, axis, route)  6.36 us
  transfers between devices with their start and end apart: 6, of which 2 were waited for; matrix products, arithmetic and copies ran while one was open for 4% of the time, Pallas kernels for 0%

commit v1 on v0

v1 whole, which is shorter than its diff:
```python
import functools

import jax
import jax.numpy as jnp
from jax import lax
from jax.experimental import pallas as pl
from jax.experimental.pallas import tpu as pltpu
from jax.sharding import PartitionSpec as P

MESH = pl.DeviceIdType.MESH
F32 = jnp.float32
BF16 = jnp.bfloat16
EPS = 0.01
LANE = 128
NB = 8
SLOTS = 64
VD = 6
MEM = 16
CH = VD * NB
ROWS = MEM * CH
ALL = ROWS + CH
PAD = 112
T_ORDER, T_FLAG, T_LAST, T_VALID, T_POS, T_LIVE, T_SIZE = 0, 64, 128, 152, 192, 256, 320


def slot_table(bi, bc, tab, cnt, first):
    base = (lax.axis_index("grid") - 1) * NB

    def clear(c, _):
        cnt[c] = 0
        return 0

    lax.fori_loop(0, 3 * NB, clear, 0)

    def count(i, _):
        s, r, k = i // (NB * 4), (i // 4) % NB, i % 4
        pos = jnp.clip(bi[s, r, k] - base, 0, 3 * NB - 1)
        tab[T_POS + i] = pos
        tab[T_LIVE + i] = (k < bc[s, r]).astype(jnp.int32)
        cnt[pos] = cnt[pos] + 1
        return 0

    lax.fori_loop(0, SLOTS, count, 0)

    def starts(c, run):
        n = cnt[c]
        tab[T_VALID + c] = jnp.minimum(n, 1)
        tab[T_LAST + c] = jnp.maximum(run + n - 1, 0)
        cnt[c] = run
        first[c] = run
        return run + n

    lax.fori_loop(0, 3 * NB, starts, jnp.int32(0))

    def place(i, _):
        pos = tab[T_POS + i]
        t = cnt[pos]
        cnt[pos] = t + 1
        tab[T_ORDER + t] = i
        tab[T_FLAG + t] = (t != first[pos]).astype(jnp.int32)
        return 0

    lax.fori_loop(0, SLOTS, place, 0)


def forward_kernel(bi, bc, lat, w_in, b_in, w_out, b_out, field, slope, tab, pf, cnt, first):
    i = pl.program_id(0)
    rows = lat.shape[0]

    @pl.when(i == 0)
    def _():
        slot_table(bi, bc, tab, cnt, first)

    x = lat[...]
    pred = jnp.zeros((rows, w_out.shape[1]), F32)
    step = 256
    c = 0.7978845608028654
    a = 0.044715
    for n in range(0, w_in.shape[1], step):
        z = jnp.dot(x, w_in[:, n : n + step], preferred_element_type=F32) + b_in[:, n : n + step]
        zz = z * z
        t = jnp.tanh(z * (c + (c * a) * zz))
        half = 0.5 + 0.5 * t
        hidden = (z * half).astype(BF16)
        d = half + (0.5 * z) * (1.0 - t * t) * (c + (3.0 * c * a) * zz)
        slope[:, n : n + step] = d.astype(BF16)
        pred += jnp.dot(hidden, w_out[n : n + step, :], preferred_element_type=F32)
    flipped = (pred + b_out[...]).T
    for b in range(rows // LANE):
        pf[pl.ds(i * (rows // LANE) + b, 96, stride=NB), :] = flipped[:, b * LANE : (b + 1) * LANE]

    @pl.when(i == pl.num_programs(0) - 1)
    def _():
        field[...] = pf[...].astype(BF16).reshape(field.shape)


def backward_kernel(z, slope, w_out, w_in, out, zf):
    i = pl.program_id(0)
    rows = slope.shape[0]

    @pl.when(i == 0)
    def _():
        zf[...] = z[...].reshape(zf.shape).astype(F32)

    parts = []
    for b in range(rows // LANE):
        parts.append(zf[pl.ds(i * (rows // LANE) + b, 96, stride=NB), :].T.astype(BF16))
    g = jnp.concatenate(parts, axis=0)
    nt = (((1,), (1,)), ((), ()))
    step = 256
    pre = []
    for n in range(0, w_in.shape[1], step):
        h = lax.dot_general(g, w_out[n : n + step, :], nt, preferred_element_type=F32)
        pre.append((h * slope[:, n : n + step].astype(F32)).astype(BF16))
    pre = jnp.concatenate(pre, axis=1)
    out[...] = lax.dot_general(pre, w_in[...], nt, preferred_element_type=F32).astype(BF16)


def score_rows(layer, v, xs, area, varw, gr, total):
    w = area[...] * varw[v]
    row = layer * ALL + v * NB

    def at(m):
        return xs[pl.ds(pl.multiple_of(row + m * CH, 8), 8), :]

    y = at(MEM)
    x = [at(m) for m in range(MEM)]
    spread = [jnp.zeros((8, LANE), F32) for _ in range(MEM)]
    pairs = jnp.zeros((8, LANE), F32)
    for m in range(MEM):
        for n in range(m + 1, MEM):
            d = x[m] - x[n]
            q = d * d + EPS
            r = lax.rsqrt(q)
            u = d * r
            pairs += q * r
            spread[m] += u
            spread[n] -= u
    misses = jnp.zeros((8, LANE), F32)
    for m in range(MEM):
        d = x[m] - y
        q = d * d + EPS
        r = lax.rsqrt(q)
        misses += q * r
        g = w * (d * r - spread[m] * (1.0 / (MEM - 1)))
        gr[pl.ds(pl.multiple_of(layer * ROWS + m * CH + v * NB, 8), 8), :] = g
    return total + w * (misses * (1.0 / MEM) - pairs * (1.0 / (MEM * (MEM - 1))))


def exchange_kernel(
    tab, varw, field, target, area, smoothers, z, part,
    recv, xs, blocks, mf, mb, gr, contrib, runs, ext, rimsend, rimrecv, fsend,
    load_sem, own_sem, send_sem, recv_sem, hsend_sem, hrecv_sem,
    rsend_sem, rrecv_sem, zsend_sem, zrecv_sem,
):
    me = lax.axis_index("member")
    g = lax.axis_index("grid")
    has_low = g > 0
    has_high = g < MEM - 1
    barrier = pltpu.get_barrier_semaphore()

    def greet(i, _):
        peer = lax.rem(me + i, MEM)
        pl.semaphore_signal(barrier, inc=1, device_id=(peer, g), device_id_type=MESH)
        return 0

    lax.fori_loop(1, MEM, greet, 0)

    @pl.when(has_low)
    def _():
        pl.semaphore_signal(barrier, inc=1, device_id=(me, g - 1), device_id_type=MESH)

    @pl.when(has_high)
    def _():
        pl.semaphore_signal(barrier, inc=1, device_id=(me, g + 1), device_id_type=MESH)

    load = pltpu.make_async_copy(smoothers, mf, load_sem)
    load.start()
    own = pltpu.make_async_copy(field.at[me], recv.at[1, me], own_sem.at[0])
    own.start()

    for b in range(NB):
        xs[pl.ds(ROWS + b, VD, stride=NB), :] = target[:, b * LANE : (b + 1) * LANE]
    recv[1, MEM] = xs[ROWS:ALL, :].astype(BF16)

    @pl.when(jnp.logical_not(has_low))
    def _():
        recv[0] = jnp.zeros(recv.shape[1:], BF16)
        rimrecv[0] = jnp.zeros(rimrecv.shape[1:], BF16)

    @pl.when(jnp.logical_not(has_high))
    def _():
        recv[2] = jnp.zeros(recv.shape[1:], BF16)
        rimrecv[1] = jnp.zeros(rimrecv.shape[1:], BF16)

    pl.semaphore_wait(
        barrier, MEM - 1 + has_low.astype(jnp.int32) + has_high.astype(jnp.int32)
    )

    def to_member(i):
        peer = lax.rem(me + i, MEM)
        return pltpu.make_async_remote_copy(
            src_ref=field.at[peer], dst_ref=recv.at[1, me],
            send_sem=send_sem.at[i], recv_sem=recv_sem.at[i],
            device_id=(peer, g), device_id_type=MESH,
        )

    def from_member(i):
        src = lax.rem(me + MEM - i, MEM)
        return pltpu.make_async_remote_copy(
            src_ref=field.at[src], dst_ref=recv.at[1, src],
            send_sem=send_sem.at[i], recv_sem=recv_sem.at[i],
            device_id=(src, g), device_id_type=MESH,
        )

    def halo(i, chunk, up):
        side, there = (0, g + 1) if up else (1, g - 1)
        return pltpu.make_async_remote_copy(
            src_ref=recv.at[1, chunk], dst_ref=recv.at[0 if up else 2, chunk],
            send_sem=hsend_sem.at[side, i], recv_sem=hrecv_sem.at[side, i],
            device_id=(me, there), device_id_type=MESH,
        )

    def pass_on(i, chunk):
        @pl.when(has_high)
        def _():
            halo(i, chunk, True).start()

        @pl.when(has_low)
        def _():
            halo(i, chunk, False).start()

    def send(i, _):
        to_member(i).start()
        return 0

    lax.fori_loop(1, MEM, send, 0)
    pass_on(MEM, MEM)
    own.wait()
    pass_on(0, me)

    load.wait()

    def weights(i, _):
        live = tab[T_LIVE + i].astype(F32)
        mb[i] = (mf[i // 32, (i // 4) % NB, i % 4] * live).astype(BF16)
        return 0

    lax.fori_loop(0, SLOTS, weights, 0)

    def arrive(i, _):
        from_member(i).wait_recv()
        pass_on(i, lax.rem(me + MEM - i, MEM))
        return 0

    lax.fori_loop(1, MEM, arrive, 0)

    xs[0:ROWS, :] = recv[1, 0:MEM].reshape(ROWS, LANE).astype(F32)
    fill = jnp.zeros((PAD - 102, LANE), BF16)
    for b in range(NB):
        blocks[NB + b] = jnp.concatenate(
            [xs[pl.ds(b, 102, stride=NB), :].astype(BF16), fill], axis=0
        )
    total = lax.fori_loop(
        0, VD, lambda v, t: score_rows(0, v, xs, area, varw, gr, t), jnp.zeros((8, LANE), F32)
    )

    def landed(i, _):
        chunk = jnp.where(i == MEM, MEM, lax.rem(me + MEM - i + MEM, MEM))

        @pl.when(has_low)
        def _():
            halo(i, chunk, True).wait_recv()

        @pl.when(has_high)
        def _():
            halo(i, chunk, False).wait_recv()

        return 0

    lax.fori_loop(0, MEM + 1, landed, 0)
    for side, first in ((0, 0), (2, 2 * NB)):
        ext[0:ALL, :] = recv[side].reshape(ALL, LANE).astype(F32)
        for b in range(NB):
            blocks[first + b] = jnp.concatenate(
                [ext[pl.ds(b, 102, stride=NB), :].astype(BF16), fill], axis=0
            )

    for s in range(2):
        for r in range(NB):
            i = (s * NB + r) * 4
            picked = jnp.concatenate([blocks[tab[T_POS + i + k]] for k in range(4)], axis=1)
            res = jnp.dot(
                picked, mb[i : i + 4].reshape(4 * LANE, LANE), preferred_element_type=F32
            )
            xs[pl.ds((s + 1) * ALL + r, 102, stride=NB), :] = res[:102]

    def later(i, t):
        return score_rows(1 + i // VD, i % VD, xs, area, varw, gr, t)

    part[...] = lax.fori_loop(0, 2 * VD, later, total)

    nt = (((1,), (1,)), ((), ()))
    for s in range(2):
        for r in range(NB):
            i = (s * NB + r) * 4
            rows = gr[pl.ds((s + 1) * ROWS + r, 96, stride=NB), :].astype(BF16)
            res = lax.dot_general(
                rows, mb[i : i + 4].reshape(4 * LANE, LANE), nt, preferred_element_type=F32
            )
            for k in range(4):
                contrib[i + k] = res[:, k * LANE : (k + 1) * LANE]

    def run(t, acc):
        acc = acc * tab[T_FLAG + t].astype(F32) + contrib[tab[T_ORDER + t]]
        runs[t] = acc
        return acc

    lax.fori_loop(0, SLOTS, run, jnp.zeros((96, LANE), F32), unroll=4)
    for c in list(range(NB)) + list(range(2 * NB, 3 * NB)) + list(range(NB, 2 * NB)):
        e = runs[tab[T_LAST + c]] * tab[T_VALID + c].astype(F32)
        ext[pl.ds((c // NB) * ROWS + c % NB, 96, stride=NB), :] = e

    def rim(q, up):
        side, there = (0, g + 1) if up else (1, g - 1)
        part4 = pl.ds(q * 4, 4)
        return pltpu.make_async_remote_copy(
            src_ref=rimsend.at[side, part4], dst_ref=rimrecv.at[side, part4],
            send_sem=rsend_sem.at[side, q], recv_sem=rrecv_sem.at[side, q],
            device_id=(me, there), device_id_type=MESH,
        )

    rimsend[1] = ext[0:ROWS, :].reshape(MEM, CH, LANE).astype(BF16)

    @pl.when(has_low)
    def _():
        for q in range(4):
            rim(q, False).start()

    rimsend[0] = ext[2 * ROWS : 3 * ROWS, :].reshape(MEM, CH, LANE).astype(BF16)

    @pl.when(has_high)
    def _():
        for q in range(4):
            rim(q, True).start()

    def to_owner(i):
        peer = lax.rem(me + i, MEM)
        return pltpu.make_async_remote_copy(
            src_ref=fsend.at[peer], dst_ref=z.at[me],
            send_sem=zsend_sem.at[i], recv_sem=zrecv_sem.at[i],
            device_id=(peer, g), device_id_type=MESH,
        )

    own_z = pltpu.make_async_copy(fsend.at[me], z.at[me], own_sem.at[1])
    for q in range(4):

        @pl.when(has_low)
        def _():
            rim(q, True).wait_recv()

        @pl.when(has_high)
        def _():
            rim(q, False).wait_recv()

        for m in range(4 * q, 4 * q + 4):
            at = m * CH
            value = gr[at : at + CH, :] + ext[ROWS + at : ROWS + at + CH, :]
            value = value + (rimrecv[0, m].astype(F32) + rimrecv[1, m].astype(F32))
            fsend[m] = value.astype(BF16)
            i = lax.rem(m - me + MEM, MEM)

            @pl.when(i > 0)
            def _():
                to_owner(i).start()

            @pl.when(i == 0)
            def _():
                own_z.start()

    own_z.wait()

    def finish(i, _):
        src = lax.rem(me + MEM - i, MEM)
        pltpu.make_async_remote_copy(
            src_ref=fsend.at[src], dst_ref=z.at[src],
            send_sem=zsend_sem.at[i], recv_sem=zrecv_sem.at[i],
            device_id=(src, g), device_id_type=MESH,
        ).wait_recv()
        to_owner(i).wait_send()
        to_member(i).wait_send()
        return 0

    lax.fori_loop(1, MEM, finish, 0)

    def sent(i, _):
        @pl.when(has_high)
        def _():
            halo(i, 0, True).wait_send()

        @pl.when(has_low)
        def _():
            halo(i, 0, False).wait_send()

        return 0

    lax.fori_loop(0, MEM + 1, sent, 0)
    for q in range(4):

        @pl.when(has_high)
        def _():
            rim(q, True).wait_send()

        @pl.when(has_low)
        def _():
            rim(q, False).wait_send()


def on_device(latents, w_in, b_in, w_out, b_out, target, area_weight, var_weight,
              smoothers, block_index, block_count):
    points = latents.shape[1]
    lat = latents.reshape(points, -1)
    width = w_in.shape[1]
    tile = 256
    whole = lambda shape: pl.BlockSpec(shape, lambda i: (0,) * len(shape))
    smem = pl.BlockSpec(memory_space=pltpu.SMEM)
    vmem = pl.BlockSpec(memory_space=pltpu.VMEM)
    anywhere = pl.BlockSpec(memory_space=pl.ANY)
    field, slope, tab = pl.pallas_call(
        forward_kernel,
        grid=(points // tile,),
        out_shape=(
            jax.ShapeDtypeStruct((MEM, CH, LANE), BF16),
            jax.ShapeDtypeStruct((points, width), BF16),
            jax.ShapeDtypeStruct((T_SIZE,), jnp.int32),
        ),
        in_specs=[
            smem, smem,
            pl.BlockSpec((tile, lat.shape[1]), lambda i: (i, 0)),
            whole(w_in.shape), whole((1, width)), whole(w_out.shape), whole((1, w_out.shape[1])),
        ],
        out_specs=(
            whole((MEM, CH, LANE)),
            pl.BlockSpec((tile, width), lambda i: (i, 0)),
            smem,
        ),
        scratch_shapes=[
            pltpu.VMEM((ROWS, LANE), F32),
            pltpu.SMEM((32,), jnp.int32),
            pltpu.SMEM((32,), jnp.int32),
        ],
        compiler_params=pltpu.CompilerParams(vmem_limit_bytes=40 * 1024 * 1024),
    )(block_index, block_count, lat, w_in, b_in.reshape(1, -1), w_out, b_out.reshape(1, -1))

    dma = pltpu.SemaphoreType.DMA
    z, part = pl.pallas_call(
        exchange_kernel,
        out_shape=(
            jax.ShapeDtypeStruct((MEM, CH, LANE), BF16),
            jax.ShapeDtypeStruct((8, LANE), F32),
        ),
        in_specs=[smem, smem, anywhere, vmem, vmem, anywhere],
        out_specs=(anywhere, vmem),
        scratch_shapes=[
            pltpu.VMEM((3, MEM + 1, CH, LANE), BF16),
            pltpu.VMEM((3 * ALL, LANE), F32),
            pltpu.VMEM((3 * NB, PAD, LANE), BF16),
            pltpu.VMEM((2, NB, 4, LANE, LANE), F32),
            pltpu.VMEM((SLOTS, LANE, LANE), BF16),
            pltpu.VMEM((3 * ROWS, LANE), F32),
            pltpu.VMEM((SLOTS, 96, LANE), F32),
            pltpu.VMEM((SLOTS, 96, LANE), F32),
            pltpu.VMEM((3 * ROWS, LANE), F32),
            pltpu.VMEM((2, MEM, CH, LANE), BF16),
            pltpu.VMEM((2, MEM, CH, LANE), BF16),
            pltpu.VMEM((MEM, CH, LANE), BF16),
            dma, dma((2,)), dma((MEM,)), dma((MEM,)), dma((2, MEM + 1)), dma((2, MEM + 1)),
            dma((2, 4)), dma((2, 4)), dma((MEM,)), dma((MEM,)),
        ],
        compiler_params=pltpu.CompilerParams(
            collective_id=0, has_side_effects=True, vmem_limit_bytes=40 * 1024 * 1024
        ),
    )(tab, var_weight, field, target, area_weight.reshape(NB, LANE), smoothers)

    grad = pl.pallas_call(
        backward_kernel,
        grid=(points // tile,),
        out_shape=jax.ShapeDtypeStruct((points, lat.shape[1]), BF16),
        in_specs=[
            whole((MEM, CH, LANE)),
            pl.BlockSpec((tile, width), lambda i: (i, 0)),
            whole(w_out.shape), whole(w_in.shape),
        ],
        out_specs=pl.BlockSpec((tile, lat.shape[1]), lambda i: (i, 0)),
        scratch_shapes=[pltpu.VMEM((ROWS, LANE), F32)],
        compiler_params=pltpu.CompilerParams(vmem_limit_bytes=40 * 1024 * 1024),
    )(z, slope, w_out, w_in)
    loss = lax.psum(jnp.sum(part), ("member", "grid")) / (3 * 96 * points * MEM)
    return grad.reshape(latents.shape), loss


def solution(mesh):
    in_specs = (
        P("member", "grid", None), P(), P(), P(), P(),
        P("member", "grid"), P("grid"), P("member"),
        P(None, "grid", None, None, None), P(None, "grid", None), P(None, "grid"),
    )
    return jax.shard_map(
        on_device, mesh=mesh, in_specs=in_specs,
        out_specs=(P("member", "grid", None), P()), check_vma=False,
    )
```

time: 266 us -> 146 us (0.55)
  waiting for transfers between devices: 67.5 us -> 0 us
  Pallas kernels: 0 us -> 46.9 us
  matrix products: 31.2 us -> 0 us
  other arithmetic: 27.4 us -> 0.6 us
  starting transfers between devices: 25.6 us -> 0 us
  local copies, waits for them, and re-layouts: 30.1 us -> 8.67 us
  blocking collectives: 78.4 us -> 86.7 us
    all_to_all x2 -> x0, waiting for transfers between devices: 67.5 us -> none  [the longest x1 38.6 us: on_device(): lax.all_to_all(jnp.stack(grads), 'member', split_axis=1, concat_axis=2, t...]
    pallas_call x0 -> x3, Pallas kernels: none -> 46.9 us  [the longest x1 30.8 us: on_device(): pl.pallas_call(exchange_kernel, out_shape=(jax.ShapeDtypeStruct((MEM, CH,...]
    dot_general x9 -> x0, matrix products: 31.2 us -> none  [the longest x1 7.86 us: on_device(): lax.dot_general(pre_grad, w_in, (((1,), (1,)), ((), ())), preferred_eleme...]
    reduce_sum x5 -> x1, other arithmetic: 19.4 us -> 0.6 us  [on_device(): loss = lax.psum(jnp.sum(part), ('member', 'grid')) / (3 * 96 * points * MEM)]
    ppermute x4 -> x0, starting transfers between devices: 13.4 us -> none  [the longest x2 6.36 us: passed_along(): return lax.ppermute(block, axis, route)]
    all_to_all x2 -> x0, starting transfers between devices: 12.1 us -> none  [the longest x1 7.72 us: on_device(): lax.all_to_all(jnp.stack(layers), 'member', split_axis=2, concat_axis=1,...]
    sub x8 -> x0, local copies, waits for them, and re-layouts: 8.97 us -> none  [the longest x6 6.25 us: ensemble_loss(): spread = fields[:, None] - fields[None, :]]
    slice x7 -> x0, local copies, waits for them, and re-layouts: 8.39 us -> none  [the longest x1 4.64 us: on_device(): joined[layer]]
  transfers between devices with their start and end apart: 6 -> 0, of which waited for: 2 -> 0; matrix products, arithmetic and copies ran while one was open for 4% -> 0% of each run, Pallas kernels for 0% -> 0%
where the time goes in v1:
time: 146 us; the launch traced here: 145 us
  blocking collectives  86.7 us (59%)
  Pallas kernels  46.9 us (32%)
  local copies, waits for them, and re-layouts  8.67 us (6%)
  between operations  2.53 us (2%)
    psum x1, blocking collectives, on_device(): loss = lax.psum(jnp.sum(part), ('member', 'grid')) / (3 * 96 * points * MEM)  86.7 us
    pallas_call x1, Pallas kernels, on_device(): pl.pallas_call(exchange_kernel, out_shape=(jax.ShapeDtypeStruct((MEM, CH,...  30.8 us
    pallas_call x1, Pallas kernels, on_device(): pl.pallas_call(forward_kernel, grid=(points // tile,), out_shape=(jax.Sha...  11.8 us
    unnamed x26, local copies, waits for them, and re-layouts  8.67 us
    pallas_call x1, Pallas kernels, on_device(): pl.pallas_call(backward_kernel, grid=(points // tile,), out_shape=jax.Sha...  4.38 us

profile of v1, /device:TPU:1, one launch (start us, length us, event | category | flops | bytes accessed | tf_op | source)
XLA Modules:
  0.0 145.5 jit_solution(5816537422329329335)
XLA Ops:
  0.6 0.8 copy.13.bi
  1.4 1.1 copy.14.w_out
  2.5 0.0 copy-start
  2.5 1.6 %copy-done = bf16[1024,1024]{1,0:T(8,128)(2,1)S(1)} copy-done((bf16[1024,1024]{1,0:T(8,128)(2,1)S(1)}, bf16[1024,1024]{1,0:T(8,128)(2,1)}, u32[]{:S(2)}) %copy-start) | copy-done | bytes 2097176
  4.1 0.0 copy-start.5
  4.1 1.6 %copy-done.5 = bf16[1,1024,1024]{2,1,0:T(8,128)(2,1)S(1)} copy-done((bf16[1,1024,1024]{2,1,0:T(8,128)(2,1)S(1)}, bf16[1,1024,1024]{2,1,0:T(8,128)(2,1)}, u32[]{:S(2)}) %copy-start.5) | copy-done | bytes 2097176
  5.7 0.7 copy-done.7
  6.4 0.7 copy-done.9
  7.1 0.7 copy-done.10
  7.7 11.8 %shard_map.122 = (bf16[16,48,128]{2,1,0:T(8,128)(2,1)S(1)}, bf16[1024,1024]{1,0:T(8,128)(2,1)S(1)}, s32[320]{0:T(512)S(1)}) custom-call(s32[2,8,4]{2,1,0:T(8,128)S(1)} %copy.13.bi, s32[2,8]{1,0:T(2,128)S(1)} %copy-done.9, bf16[1024,1024]{1,0:T(8,128)(2,1)S(1)} %bitcast.5, bf16[1024,1024]{1,0:T(8,128)(2,1)S(1)} %copy-done, f32[1,1024]{1,0:T(1,128)S(1)} %bitcast.6, ...), custom_call_target="tpu_custom_call" | custom-call | tf_op jit(solution)/shard_map/pallas_call | solution.py:429
  19.5 0.0 copy-start.3
  19.5 0.0 copy-done.2
  19.5 0.0 copy-done.6
  19.5 0.0 copy-done.8
  19.6 0.0 copy-done.11
  19.6 0.0 copy-start.1
  19.6 30.8 %shard_map.123 = (bf16[16,48,128]{2,1,0:T(8,128)(2,1)S(1)}, f32[8,128]{1,0:T(8,128)S(1)}) custom-call(s32[320]{0:T(512)S(1)} %get-tuple-element.7.tab, f32[6]{0:T(128)S(1)} %copy-done.11, bf16[16,48,128]{2,1,0:T(8,128)(2,1)S(1)} %get-tuple-element.8.field, f32[6,1024]{1,0:T(8,128)S(1)} %copy-done.6, f32[8,128]{1,0:T(8,128)S(1)} %bitcast.7, ...), custom_call_target="tpu_custom_call" | custom-call | tf_op jit(solution)/shard_map/pallas_call | solution.py:456
  50.4 0.0 copy-done.3
  50.4 0.6 reduce_sum.9
  51.0 86.7 %psum.7 = f32[]{:T(128)} all-reduce(f32[]{:T(128)} %reduce_sum.9), channel_id=1, replica_groups=mesh['member'=16,'grid'=16] {'member','grid'}, use_global_device_ids=true, to_apply=%region_1.0 | all-reduce | flops 1 | bytes 8 | tf_op jit(solution)/shard_map/psum | solution.py:498
  138.3 0.0 copy-done.1
  138.4 0.0 copy-start.4
  138.4 1.6 %copy-done.4 = bf16[1024,1024]{1,0:T(8,128)(2,1)S(1)} copy-done((bf16[1024,1024]{1,0:T(8,128)(2,1)S(1)}, bf16[1024,1024]{1,0:T(8,128)(2,1)}, u32[]{:S(2)}) %copy-start.4) | copy-done | bytes 2097176
  139.9 4.4 %shard_map.124 = bf16[1024,1024]{1,0:T(8,128)(2,1)} custom-call(bf16[16,48,128]{2,1,0:T(8,128)(2,1)S(1)} %get-tuple-element.9.z, bf16[1024,1024]{1,0:T(8,128)(2,1)S(1)} %copy-done.4, bf16[1024,96]{1,0:T(8,128)(2,1)S(1)} %copy.14.w_out, bf16[1024,1024]{1,0:T(8,128)(2,1)S(1)} %copy-done.1), custom_call_target="tpu_custom_call" | custom-call | tf_op jit(solution)/shard_map/pallas_call | solution.py:485
  (7 shorter events, 0.0 us)
Async XLA Ops:
  2.5 1.6 %copy-start = (bf16[1024,1024]{1,0:T(8,128)(2,1)S(1)}, bf16[1024,1024]{1,0:T(8,128)(2,1)}, u32[]{:S(2)}) copy-start(bf16[1024,1024]{1,0:T(8,128)(2,1)} %w_in.3) | copy-start | bytes 6291460
  4.1 1.6 %copy-start.5 = (bf16[1,1024,1024]{2,1,0:T(8,128)(2,1)S(1)}, bf16[1,1024,1024]{2,1,0:T(8,128)(2,1)}, u32[]{:S(2)}) copy-start(bf16[1,1024,1024]{2,1,0:T(8,128)(2,1)} %param.11) | copy-start | bytes 6291460
  5.7 0.7 copy-start.7
  6.4 0.7 copy-start.9
  7.1 0.7 copy-start.10
  7.7 11.8 %copy-start.2 = (f32[2,8,4,128,128]{4,3,2,1,0:T(8,128)S(1)}, f32[2,8,4,128,128]{4,3,2,1,0:T(8,128)}, u32[]{:S(2)}) copy-start(f32[2,8,4,128,128]{4,3,2,1,0:T(8,128)} %smoothers.1) | copy-start | bytes 12582916
  7.7 11.8 %copy-start.6 = (f32[6,1024]{1,0:T(8,128)S(1)}, f32[6,1024]{1,0:T(8,128)}, u32[]{:S(2)}) copy-start(f32[6,1024]{1,0:T(8,128)} %target.1) | copy-start | bytes 73732
  7.7 11.8 %copy-start.8 = (f32[1024]{0:T(1024)S(1)}, f32[1024]{0:T(1024)}, u32[]{:S(2)}) copy-start(f32[1024]{0:T(1024)} %param.17) | copy-start | bytes 12292
  7.7 11.8 %copy-start.11 = (f32[6]{0:T(128)S(1)}, f32[6]{0:T(128)}, u32[]{:S(2)}) copy-start(f32[6]{0:T(128)} %varw.1) | copy-start | bytes 76
  19.5 30.9 %copy-start.3 = (bf16[1024,1024]{1,0:T(8,128)(2,1)}, bf16[1024,1024]{1,0:T(8,128)(2,1)S(1)}, u32[]{:S(2)}) copy-start(bf16[1024,1024]{1,0:T(8,128)(2,1)S(1)} %get-tuple-element.10.slope) | copy-start | bytes 6291460
  19.6 118.8 %copy-start.1 = (bf16[1024,1024]{1,0:T(8,128)(2,1)S(1)}, bf16[1024,1024]{1,0:T(8,128)(2,1)}, u32[]{:S(2)}) copy-start(bf16[1024,1024]{1,0:T(8,128)(2,1)} %w_in.3) | copy-start | bytes 6291460
  138.4 1.6 %copy-start.4 = (bf16[1024,1024]{1,0:T(8,128)(2,1)S(1)}, bf16[1024,1024]{1,0:T(8,128)(2,1)}, u32[]{:S(2)}) copy-start(bf16[1024,1024]{1,0:T(8,128)(2,1)} %copy-done.3) | copy-start | bytes 6291460
